TPU v7x, 32 devices: a whole 2x2x4 slice. The times are simulated.
32 devices in a mesh: row: 4 (over y, core), col: 2 (over x), depth: 4 (over z).
Axes of the slice: x: 2, y: 2, z: 4, core: 2. Of those that a mesh axis runs over, the one named last changes fastest.
Arguments:
- density: bfloat16 [2048, 2048], P('row', 'col'), may hold values from -0.125 to 0.125
- pattern: int32 [32, 32], P('row', 'col'), may hold values 0 or 1
Outputs:
- square: bfloat16 [2048, 2048], P(('row', 'depth'), 'col')
All inputs are finite; a program needn't handle non-finite values. No bound on the sum of `pattern` on one device may be relied on, other than what follows from the above.
Results may differ from a plain program's by a relative error of at most 0.001.
Values may be sent and summed in bfloat16 or wider, within the bound.
A program may use at most 64 MiB of HBM per device.

v0:
```python
import jax
import jax.numpy as jnp
from jax import lax
from jax.sharding import PartitionSpec as P

BLK = 64


def expand(blocks):
    return jnp.repeat(jnp.repeat(blocks, BLK, axis=0), BLK, axis=1)


def shards(density, pattern):
    cols_here = density.shape[1]
    depth_count = lax.axis_size("depth")
    layer = lax.axis_index("depth")
    masked = jnp.where(expand(pattern) > 0, density, jnp.zeros_like(density))
    slab = lax.all_gather(masked, "col", axis=1, tiled=True)
    width = cols_here // depth_count
    column_part = lax.dynamic_slice_in_dim(masked, layer * width, width, 1)
    partial_cols = jnp.dot(
        slab,
        lax.all_gather(column_part, "row", axis=0, tiled=True),
        preferred_element_type=jnp.float32,
    )
    quarter = pattern.shape[1] // depth_count
    local_mask = lax.dynamic_slice_in_dim(pattern, layer * quarter, quarter, 1)
    filtered = jnp.where(expand(local_mask) > 0, partial_cols, jnp.zeros_like(partial_cols))
    return lax.all_to_all(
        filtered.astype(jnp.bfloat16), "depth", split_axis=0, concat_axis=1, tiled=True
    )


def solution(mesh):
    return jax.shard_map(
        shards,
        mesh=mesh,
        in_specs=(P("row", "col"), P("row", "col")),
        out_specs=P(("row", "depth"), "col"),
        check_vma=False,
    )
```

profile of v0, /device:TPU:0, one launch (start us, length us, event | category | flops | bytes accessed | tf_op | source)
XLA Modules:
  0.0 87.7 jit_solution(12565676332818657641)
XLA Ops:
  6.5 0.0 all-gather.5.cloned.1.call-start
  6.5 0.7 broadcast_compare_fusion
  7.2 0.1 copy.5
  7.3 0.1 broadcast_in_dim.20
  7.4 0.1 gt.34
  7.5 1.5 %copy.6 = bf16[512,1024]{0,1:T(8,128)(2,1)S(1)} copy(bf16[512,1024]{1,0:T(8,128)(2,1)} %param.2) | data formatting | bytes 2097152 | tf_op args[0]
  9.0 0.0 copy-start.1
  9.0 0.1 bitcast_select_fusion
  9.1 0.0 copy-start
  9.1 0.8 constant_dynamic-slice_fusion
  9.9 0.0 all-gather.5.cloned.1.call-update
  10.0 0.0 all-gather.3.cloned.1.call-start
  10.0 0.2 copy-done
  10.2 0.5 all-gather.3.cloned.1.call-update
  10.7 0.0 copy-done.1
  10.7 0.1 dynamic-slice_compare_fusion
  10.8 0.1 copy.4
  10.9 0.1 broadcast_in_dim.18
  11.0 0.1 gt.30
  11.1 0.2 copy.7
  11.4 18.2 %all-gather.5.cloned.1.call-done = bf16[2048,256]{0,1:T(8,128)(2,1)} async-done(((bf16[512,256]{0,1:T(8,128)(2,1)}), bf16[2048,256]{0,1:T(8,128)(2,1)}) %all-gather.5.cloned.1.call-update) | async-done | bytes 1048592 | tf_op jit(solution)/shard_map/all_gather | solution.py:23
  29.6 34.7 %all-gather.3.cloned.1.call-done = bf16[512,2048]{0,1:T(8,128)(2,1)} async-done(((bf16[512,1024]{0,1:T(8,128)(2,1)}), bf16[512,2048]{0,1:T(8,128)(2,1)}) %all-gather.3.cloned.1.call-update) | async-done | bytes 2097168 | tf_op jit(solution)/shard_map/all_gather | solution.py:18
  64.2 2.6 %fusion = bf16[512,256]{1,0:T(8,128)(2,1)S(1)} fusion(pred[512,256]{1,0:T(32,128)(4,1)S(1)} %copy.7, bf16[512,2048]{0,1:T(8,128)(2,1)} %all-gather.3.cloned.1.call-done, bf16[2048,256]{0,1:T(8,128)(2,1)} %all-gather.5.cloned.1.call-done), kind=kOutput, calls=%fused_computation.2 | convolution fusion | flops 537133056 | bytes 3538944 | tf_op jit(solution)/shard_map/dot_general | solution.py:21
  66.9 13.3 %all_to_all.19 = bf16[4,128,256]{2,1,0:T(8,128)(2,1)S(1)} all-to-all(bf16[4,128,256]{2,1,0:T(8,128)(2,1)S(1)} %bitcast.15), channel_id=1, replica_groups=mesh['row'=4,'col'=2,'depth'=4] {'depth'}, dimensions={0} | all-to-all | bytes 524288 | tf_op jit(solution)/shard_map/all_to_all | solution.py:29
  80.1 0.7 copy.9
  (1 shorter events, 0.0 us)
Async XLA Ops:
  6.5 23.0 %all-gather.5.cloned.1.call-start = ((), (), s32[]{:S(2)}) async-start(), calls=%async_computation.2 | async-start | bytes 1310720 | tf_op jit(solution)/shard_map/all_gather | solution.py:23
  9.0 1.7 %copy-start.1 = (s32[8,16]{1,0:T(8,128)S(1)}, s32[8,16]{1,0:T(8,128)}, u32[]{:S(2)}) copy-start(s32[8,16]{1,0:T(8,128)} %param.3) | copy-start | bytes 1540
  9.1 1.1 %copy-start = (bf16[512,1024]{0,1:T(8,128)(2,1)}, bf16[512,1024]{0,1:T(8,128)(2,1)S(1)}, u32[]{:S(2)}) copy-start(bf16[512,1024]{0,1:T(8,128)(2,1)S(1)} %bitcast_select_fusion) | copy-start | bytes 3145732
  10.0 54.3 %all-gather.3.cloned.1.call-start = ((), (), s32[]{:S(2)}) async-start(), calls=%async_computation.1 | async-start | bytes 3145728 | tf_op jit(solution)/shard_map/all_gather | solution.py:18
Sparse Core Ops, SparseCore 0:
  10.1 19.4 all-gather.4
  31.1 33.0 all-gather.2
where the time goes:
time: 87.9 us; the launch traced here: 87.7 us
  waiting for transfers between devices  53.4 us (61%)
  between operations  13.5 us (15%)
  blocking collectives  13.3 us (15%)
  local copies, waits for them, and re-layouts  4.01 us (5%)
  matrix products  2.6 us (3%)
    all_gather x1, waiting for transfers between devices, shards(): slab = lax.all_gather(masked, 'col', axis=1, tiled=True)  34.7 us
    all_gather x1, waiting for transfers between devices, shards(): lax.all_gather(column_part, 'row', axis=0, tiled=True)  18.2 us
    all_to_all x1, blocking collectives, shards(): lax.all_to_all(filtered.astype(jnp.bfloat16), 'depth', split_axis=0, conc...  13.3 us
    dot_general x1, matrix products, shards(): jnp.dot(slab, lax.all_gather(column_part, 'row', axis=0, tiled=True), pre...  2.6 us
  transfers between devices with their start and end apart: 2, of which 2 were waited for; matrix products, arithmetic and copies ran while one was open for 1% of the time, Pallas kernels for 0%

commit v1 on v0

v1 whole, which is shorter than its diff:
```python
import functools

import jax
import jax.numpy as jnp
from jax import lax
from jax.experimental import pallas as pl
from jax.experimental.pallas import tpu as pltpu
from jax.sharding import PartitionSpec as P

BLK = 64
UNIT = 128
MESH = pl.DeviceIdType.MESH
SIXTEENTHS = (4, 4, 3, 3, 1, 1)


def kernel(
    n_row, n_col, n_depth,
    density, pattern, out,
    raw, cols, left, mask, acc,
    load_sem, x_send, x_recv, y_send, y_recv, z_send, z_recv, own_send, own_recv,
    s_send, s_recv,
):
    rows, width = density.shape
    strip = rows // n_depth
    cores = 2 if n_row % 2 == 0 else 1
    share = 2 if n_depth % 2 == 0 else 1
    n_y = n_row // cores
    part = rows // share
    sizes = [s * (part // 16) for s in SIXTEENTHS]
    starts = [sum(sizes[:i]) for i in range(len(sizes))]
    chunks = len(sizes)
    row, col, depth = lax.axis_index("row"), lax.axis_index("col"), lax.axis_index("depth")
    y, core = row // cores, row % cores
    half = depth % share
    sibling = y * cores + (cores - 1 - core)
    mate = depth - half + (share - 1 - half)

    def y_at(j):
        return lax.rem(y + j, n_y)

    here = (row, col, depth)
    y_peers = [(y_at(j) * cores + core, col, depth) for j in range(1, n_y)]
    x_peers = [(row, lax.rem(col + j, n_col), depth) for j in range(1, n_col)]
    sib = (sibling, col, depth)
    mate_at = (row, col, mate)
    greeted = y_peers + x_peers + [sib] * (cores > 1) + [mate_at] * (share > 1)

    barrier = pltpu.get_barrier_semaphore()
    for peer in greeted:
        pl.semaphore_signal(barrier, inc=1, device_id=peer, device_id_type=MESH)

    load = pltpu.make_async_copy(density, raw, load_sem)
    load.start()

    block_rows, block_cols = pattern.shape
    low = lax.broadcasted_iota(jnp.int32, (block_cols, width), 0) * BLK
    at = lax.broadcasted_iota(jnp.int32, (block_cols, width), 1)
    spread = jnp.where((at >= low) & (at < low + BLK), 1.0, 0.0).astype(jnp.bfloat16)
    mask[...] = jnp.dot(
        pattern[...].astype(jnp.float32).astype(jnp.bfloat16), spread,
        preferred_element_type=jnp.float32,
    )
    load.wait()
    base = pl.multiple_of(row * rows, rows)
    for i in range(block_rows):
        keep = jnp.broadcast_to(mask[i:i + 1, :], (16, width)).astype(jnp.bfloat16)
        for t in range(BLK // 16):
            lo = i * BLK + t * 16
            cols[pl.ds(base + lo, 16), :] = raw[lo:lo + 16, :] * keep
    units_here = width // UNIT
    mine = cols[pl.ds(pl.multiple_of(base + depth * strip, strip), strip), :]
    for u in range(units_here):
        left[col * units_here + u] = mine[:, u * UNIT:(u + 1) * UNIT]

    pl.semaphore_wait(barrier, len(greeted))

    def copy(src, dst, send, recv, to):
        return pltpu.make_async_remote_copy(
            src_ref=src, dst_ref=dst, send_sem=send, recv_sem=recv,
            device_id=to, device_id_type=MESH,
        )

    def piece(r, h, i):
        begin = pl.multiple_of(r * rows + h * part + starts[i], 16)
        return cols.at[pl.ds(begin, sizes[i]), :]

    sent = []
    for i in range(chunks):
        for j in range(1, n_y):
            c = copy(piece(row, half, i), piece(row, half, i),
                     y_send.at[j - 1, i], y_recv.at[j - 1, i], y_peers[j - 1])
            c.start()
            sent.append(c)
    for j in range(1, n_col):
        ref = left.at[pl.ds(col * units_here, units_here)]
        c = copy(ref, ref, x_send.at[j - 1], x_recv.at[j - 1], x_peers[j - 1])
        c.start()
        sent.append(c)
    if cores > 1:
        ref = cols.at[pl.ds(base, rows), :]
        c = copy(ref, ref, own_send, own_recv, sib)
        c.start()
        sent.append(c)

    def arrived(ref, recv):
        copy(ref, ref, own_send, recv, sib).wait_recv()

    def to_sibling(j, h, w, i, r):
        if cores > 1:
            c = copy(piece(r, h, i), piece(r, h, i),
                     s_send.at[j - 1, w, i], s_recv.at[j - 1, w, i], sib)
            c.start()
            sent.append(c)

    def multiply(starts_at):
        total = None
        for begin in starts_at:
            term = jnp.dot(
                left[begin // UNIT],
                cols[pl.ds(pl.multiple_of(begin, UNIT), UNIT), :],
                preferred_element_type=jnp.float32,
            )
            total = term if total is None else total + term
        return total

    def from_y(j):
        return lax.rem(y + n_y - j, n_y)

    def take_y(j, i):
        r = from_y(j) * cores + core
        arrived(piece(r, half, i), y_recv.at[j - 1, i])
        if share > 1:
            c = copy(piece(r, half, i), piece(r, half, i),
                     z_send.at[j - 1, i], z_recv.at[j - 1, i], mate_at)
            c.start()
            sent.append(c)
        to_sibling(j, half, 0, i, r)

    def take_z(j, i):
        if share > 1:
            r = from_y(j) * cores + core
            arrived(piece(r, 1 - half, i), z_recv.at[j - 1, i])
            to_sibling(j, 1 - half, 1, i, r)

    def take_sibling(j, w, i):
        if cores > 1:
            r = from_y(j) * cores + (cores - 1 - core)
            h = half if w == 0 else 1 - half
            arrived(piece(r, h, i), s_recv.at[j - 1, w, i])

    def finish(first, last):
        lo = starts[first] if first < chunks else part
        hi = starts[last] if last < chunks else part
        for i in range(first, last):
            for j in range(1, n_y):
                for w in range(share):
                    take_sibling(j, w, i)
        for j in range(1, n_y):
            begins = []
            for k in range(cores):
                for h in range(share):
                    begins += [(from_y(j) * cores + k) * rows + h * part + q
                               for q in range(lo, hi, UNIT)]
            acc[...] += multiply(begins)

    cut = next(i for i in range(chunks) if starts[i] == part // 2)
    for i in range(chunks):
        for j in range(1, n_y):
            take_y(j, i)
            if i:
                take_z(j, i - 1)
        if i == cut:
            for j in range(1, n_col):
                c = lax.rem(col + n_col - j, n_col)
                arrived(left.at[pl.ds(c * units_here, units_here)], x_recv.at[j - 1])
            if cores > 1:
                arrived(cols.at[pl.ds(sibling * rows, rows), :], own_recv)
            acc[...] = multiply([(y * cores + k) * rows + q
                                 for k in range(cores) for q in range(0, rows, UNIT)])
        if i == cut + 1:
            finish(0, cut)
    for j in range(1, n_y):
        take_z(j, chunks - 1)
    if cut + 1 >= chunks:
        finish(0, cut)
    finish(cut, chunks)

    for b in range(strip // BLK):
        keep = mask[pl.ds(depth * (strip // BLK) + b, 1), :]
        out[b * BLK:(b + 1) * BLK, :] = (acc[b * BLK:(b + 1) * BLK, :] * keep).astype(out.dtype)
    for c in sent:
        c.wait_send()


def shards(n_row, n_col, n_depth, density, pattern):
    rows, width = density.shape
    strip = rows // n_depth
    n_y = n_row // 2 if n_row % 2 == 0 else n_row
    chunks = len(SIXTEENTHS)
    dma = pltpu.SemaphoreType.DMA
    j = max(n_y - 1, 1)
    return pl.pallas_call(
        functools.partial(kernel, n_row, n_col, n_depth),
        out_shape=jax.ShapeDtypeStruct((strip, width), jnp.bfloat16),
        in_specs=[pl.BlockSpec(memory_space=pl.ANY), pl.BlockSpec(memory_space=pltpu.VMEM)],
        out_specs=pl.BlockSpec(memory_space=pltpu.VMEM),
        scratch_shapes=[
            pltpu.VMEM((rows, width), jnp.bfloat16),
            pltpu.VMEM((n_row * rows, width), jnp.bfloat16),
            pltpu.VMEM((n_col * width // UNIT, strip, UNIT), jnp.bfloat16),
            pltpu.VMEM((pattern.shape[0], width), jnp.float32),
            pltpu.VMEM((strip, width), jnp.float32),
            dma(()),
            dma((max(n_col - 1, 1),)), dma((max(n_col - 1, 1),)),
            dma((j, chunks)), dma((j, chunks)),
            dma((j, chunks)), dma((j, chunks)),
            dma(()), dma(()),
            dma((j, 2, chunks)), dma((j, 2, chunks)),
        ],
        compiler_params=pltpu.CompilerParams(
            collective_id=0, has_side_effects=True, vmem_limit_bytes=32 * 1024 * 1024
        ),
    )(density, pattern)


def solution(mesh):
    sizes = [mesh.shape[name] for name in ("row", "col", "depth")]
    return jax.shard_map(
        functools.partial(shards, *sizes),
        mesh=mesh,
        in_specs=(P("row", "col"), P("row", "col")),
        out_specs=P(("row", "depth"), "col"),
        check_vma=False,
    )
```

time: 87.9 us -> 29.8 us (0.34)
  waiting for transfers between devices: 53.4 us -> 0 us
  Pallas kernels: 0 us -> 26.6 us
  between operations: 13.5 us -> 0.01 us
  blocking collectives: 13.3 us -> 0 us
  matrix products: 2.6 us -> 0 us
  local copies, waits for them, and re-layouts: 4.01 us -> 2.62 us
    all_gather x2 -> x0, waiting for transfers between devices: 52.9 us -> none  [the longest x1 34.7 us: shards(): slab = lax.all_gather(masked, 'col', axis=1, tiled=True)]
    pallas_call x0 -> x1, Pallas kernels: none -> 26.6 us  [shards(): pl.pallas_call(functools.partial(kernel, n_row, n_col, n_depth), out_shap...]
    all_to_all x1 -> x0, blocking collectives: 13.3 us -> none  [shards(): lax.all_to_all(filtered.astype(jnp.bfloat16), 'depth', split_axis=0, conc...]
    dot_general x1 -> x0, matrix products: 2.6 us -> none  [shards(): jnp.dot(slab, lax.all_gather(column_part, 'row', axis=0, tiled=True), pre...]
    unnamed x5, local copies, waits for them, and re-layouts: 1.67 us -> 2.62 us
  transfers between devices with their start and end apart: 2 -> 0, of which waited for: 2 -> 0; matrix products, arithmetic and copies ran while one was open for 1% -> 0% of each run, Pallas kernels for 0% -> 0%
where the time goes in v1:
time: 29.8 us; the launch traced here: 29.3 us
  Pallas kernels  26.6 us (89%)
  local copies, waits for them, and re-layouts  2.62 us (9%)
    pallas_call x1, Pallas kernels, shards(): pl.pallas_call(functools.partial(kernel, n_row, n_col, n_depth), out_shap...  26.6 us
    unnamed x5, local copies, waits for them, and re-layouts  2.62 us

profile of v1, /device:TPU:0, one launch (start us, length us, event | category | flops | bytes accessed | tf_op | source)
XLA Modules:
  0.0 29.3 jit_solution(4419846403872709692)
XLA Ops:
  0.0 0.0 copy-start
  0.0 1.2 %copy-done = bf16[512,1024]{1,0:T(8,128)(2,1)S(1)} copy-done((bf16[512,1024]{1,0:T(8,128)(2,1)S(1)}, bf16[512,1024]{1,0:T(8,128)(2,1)}, u32[]{:S(2)}) %copy-start) | copy-done | bytes 1048600
  1.2 0.0 copy-start.1
  1.2 0.7 %copy-done.1 = s32[8,16]{1,0:T(8,128)S(1)} copy-done((s32[8,16]{1,0:T(8,128)S(1)}, s32[8,16]{1,0:T(8,128)}, u32[]{:S(2)}) %copy-start.1) | copy-done | bytes 536
  1.9 26.6 %shard_map.28 = bf16[128,1024]{1,0:T(8,128)(2,1)S(1)} custom-call(bf16[512,1024]{1,0:T(8,128)(2,1)S(1)} %copy-done, s32[8,16]{1,0:T(8,128)S(1)} %copy-done.1), custom_call_target="tpu_custom_call" | custom-call | tf_op jit(solution)/shard_map/pallas_call | solution.py:202
  28.6 0.7 %copy.4 = bf16[128,1024]{1,0:T(8,128)(2,1)} copy(bf16[128,1024]{1,0:T(8,128)(2,1)S(1)} %shard_map.28) | data formatting | bytes 524288
Async XLA Ops:
  0.0 1.2 %copy-start = (bf16[512,1024]{1,0:T(8,128)(2,1)S(1)}, bf16[512,1024]{1,0:T(8,128)(2,1)}, u32[]{:S(2)}) copy-start(bf16[512,1024]{1,0:T(8,128)(2,1)} %density.1) | copy-start | bytes 3145732
  1.2 0.7 %copy-start.1 = (s32[8,16]{1,0:T(8,128)S(1)}, s32[8,16]{1,0:T(8,128)}, u32[]{:S(2)}) copy-start(s32[8,16]{1,0:T(8,128)} %pattern.1) | copy-start | bytes 1540

commit v2 on v1

--- a/solution.py
+++ b/solution.py
@@ -10,14 +10,14 @@
 BLK = 64
 UNIT = 128
 MESH = pl.DeviceIdType.MESH
-SIXTEENTHS = (4, 4, 3, 3, 1, 1)
+SIXTEENTHS = (4, 4, 4, 4)
 
 
 def kernel(
     n_row, n_col, n_depth,
     density, pattern, out,
-    raw, cols, left, mask, acc,
-    load_sem, x_send, x_recv, y_send, y_recv, z_send, z_recv, own_send, own_recv,
+    raw, blocks, cols, left, mask, acc,
+    load_sem, blocks_sem, x_send, x_recv, y_send, y_recv, z_send, z_recv, own_send, own_recv,
     s_send, s_recv,
 ):
     rows, width = density.shape
@@ -45,6 +45,8 @@
     mate_at = (row, col, mate)
     greeted = y_peers + x_peers + [sib] * (cores > 1) + [mate_at] * (share > 1)
 
+    fetch = pltpu.make_async_copy(pattern, blocks, blocks_sem)
+    fetch.start()
     barrier = pltpu.get_barrier_semaphore()
     for peer in greeted:
         pl.semaphore_signal(barrier, inc=1, device_id=peer, device_id_type=MESH)
@@ -56,8 +58,9 @@
     low = lax.broadcasted_iota(jnp.int32, (block_cols, width), 0) * BLK
     at = lax.broadcasted_iota(jnp.int32, (block_cols, width), 1)
     spread = jnp.where((at >= low) & (at < low + BLK), 1.0, 0.0).astype(jnp.bfloat16)
+    fetch.wait()
     mask[...] = jnp.dot(
-        pattern[...].astype(jnp.float32).astype(jnp.bfloat16), spread,
+        blocks[...].astype(jnp.float32).astype(jnp.bfloat16), spread,
         preferred_element_type=jnp.float32,
     )
     load.wait()
@@ -202,15 +205,16 @@
     return pl.pallas_call(
         functools.partial(kernel, n_row, n_col, n_depth),
         out_shape=jax.ShapeDtypeStruct((strip, width), jnp.bfloat16),
-        in_specs=[pl.BlockSpec(memory_space=pl.ANY), pl.BlockSpec(memory_space=pltpu.VMEM)],
+        in_specs=[pl.BlockSpec(memory_space=pltpu.HBM), pl.BlockSpec(memory_space=pltpu.HBM)],
         out_specs=pl.BlockSpec(memory_space=pltpu.VMEM),
         scratch_shapes=[
             pltpu.VMEM((rows, width), jnp.bfloat16),
+            pltpu.VMEM(pattern.shape, jnp.int32),
             pltpu.VMEM((n_row * rows, width), jnp.bfloat16),
             pltpu.VMEM((n_col * width // UNIT, strip, UNIT), jnp.bfloat16),
             pltpu.VMEM((pattern.shape[0], width), jnp.float32),
             pltpu.VMEM((strip, width), jnp.float32),
-            dma(()),
+            dma(()), dma(()),
             dma((max(n_col - 1, 1),)), dma((max(n_col - 1, 1),)),
             dma((j, chunks)), dma((j, chunks)),
             dma((j, chunks)), dma((j, chunks)),
@@ -218,7 +222,7 @@
             dma((j, 2, chunks)), dma((j, 2, chunks)),
         ],
         compiler_params=pltpu.CompilerParams(
-            collective_id=0, has_side_effects=True, vmem_limit_bytes=32 * 1024 * 1024
+            collective_id=0, has_side_effects=True, vmem_limit_bytes=60 * 1024 * 1024
         ),
     )(density, pattern)
 

time: 29.8 us -> 26 us (0.87)
  Pallas kernels: 26.6 us -> 23.8 us
  local copies, waits for them, and re-layouts: 2.62 us -> 1.67 us
    pallas_call x1, Pallas kernels: 26.6 us -> 23.8 us  [shards(): pl.pallas_call(functools.partial(kernel, n_row, n_col, n_depth), out_shap...]
    unnamed x5 -> x1, local copies, waits for them, and re-layouts: 2.62 us -> 1.67 us
where the time goes in v2:
time: 26 us; the launch traced here: 25.4 us
  Pallas kernels  23.8 us (92%)
  local copies, waits for them, and re-layouts  1.67 us (6%)
    pallas_call x1, Pallas kernels, shards(): pl.pallas_call(functools.partial(kernel, n_row, n_col, n_depth), out_shap...  23.8 us
    unnamed x1, local copies, waits for them, and re-layouts  1.67 us

profile of v2, /device:TPU:0, one launch (start us, length us, event | category | flops | bytes accessed | tf_op | source)
XLA Modules:
  0.0 25.4 jit_solution(9230082611604802407)
XLA Ops:
  0.0 23.8 %shard_map.28 = bf16[128,1024]{1,0:T(8,128)(2,1)} custom-call(bf16[512,1024]{1,0:T(8,128)(2,1)} %density.1, s32[8,16]{1,0:T(8,128)} %pattern.1), custom_call_target="tpu_custom_call" | custom-call | tf_op jit(solution)/shard_map/pallas_call | solution.py:205
  23.8 1.7 %copy.4 = bf16[128,1024]{1,0:T(8,128)(2,1)} copy(bf16[128,1024]{1,0:T(8,128)(2,1)} %shard_map.28) | data formatting | bytes 524288

commit v3 on v0

v3 whole, which is shorter than its diff:
```python
import functools

import jax
import jax.numpy as jnp
from jax import lax
from jax.experimental import pallas as pl
from jax.experimental.pallas import tpu as pltpu
from jax.sharding import PartitionSpec as P

BLK = 64
LANES = 128
STEPS = 2
AHEAD = 2
MESH = pl.DeviceIdType.MESH


def layout(n_row, n_depth):
    cores = 2 if n_row % 2 == 0 else 1
    share = 2 if n_depth % 2 == 0 else 1
    return cores, share, n_row // cores


def kernel(
    n_row, n_col, n_depth,
    density, pattern, out,
    raw_cols, raw_left, blocks, cols, left, mask, mask_tiles, given, made,
    load_sem, x_send, x_recv, y_send, y_recv, z_send, z_recv, own_send, own_recv,
    s_send, s_recv, o_send, o_recv,
):
    rows, width = density.shape
    strip = rows // n_depth
    cores, share, n_y = layout(n_row, n_depth)
    pair = strip * share
    tiles = width // share // LANES
    row, col, depth = lax.axis_index("row"), lax.axis_index("col"), lax.axis_index("depth")
    y, core = row // cores, row % cores
    half = depth % share
    sibling = y * cores + (cores - 1 - core)
    mate = depth - half + (share - 1 - half)

    y_peers = [(lax.rem(y + j, n_y) * cores + core, col, depth) for j in range(1, n_y)]
    x_peers = [(row, lax.rem(col + j, n_col), depth) for j in range(1, n_col)]
    sib = (sibling, col, depth)
    mate_at = (row, col, mate)
    greeted = y_peers + x_peers + [sib] * (cores > 1) + [mate_at] * (share > 1)

    pair_base = pl.multiple_of((depth - half) * strip, pair)
    loads = [pltpu.make_async_copy(pattern, blocks, load_sem.at[0])]
    for t in range(tiles):
        lane = pl.multiple_of((half * tiles + t) * LANES, LANES)
        loads.append(pltpu.make_async_copy(
            density.at[:, pl.ds(lane, LANES)], raw_cols.at[t], load_sem.at[1 + t]))
    loads.append(pltpu.make_async_copy(
        density.at[pl.ds(pair_base, pair), :], raw_left, load_sem.at[1 + tiles]))
    for c in loads:
        c.start()
    barrier = pltpu.get_barrier_semaphore()
    for peer in greeted:
        pl.semaphore_signal(barrier, inc=1, device_id=peer, device_id_type=MESH)

    block_rows, block_cols = pattern.shape
    low = lax.broadcasted_iota(jnp.int32, (block_cols, width), 0) * BLK
    at = lax.broadcasted_iota(jnp.int32, (block_cols, width), 1)
    spread = jnp.where((at >= low) & (at < low + BLK), 1.0, 0.0).astype(jnp.bfloat16)
    loads[0].wait()
    wide = jnp.dot(
        blocks[...].astype(jnp.float32).astype(jnp.bfloat16), spread,
        preferred_element_type=jnp.float32,
    )
    mask[...] = wide
    for t in range(share * tiles):
        mask_tiles[t] = wide[:, t * LANES:(t + 1) * LANES]
    base = pl.multiple_of(row * rows, rows)
    for t in range(tiles):
        loads[1 + t].wait()
        for i in range(block_rows):
            keep = mask_tiles[half * tiles + t, i:i + 1, :]
            keep = jnp.broadcast_to(keep, (BLK, LANES)).astype(jnp.bfloat16)
            cols[t, pl.ds(base + i * BLK, BLK), :] = raw_cols[t, i * BLK:(i + 1) * BLK, :] * keep

    pl.semaphore_wait(barrier, len(greeted))

    def copy(src, dst, send, recv, to):
        return pltpu.make_async_remote_copy(
            src_ref=src, dst_ref=dst, send_sem=send, recv_sem=recv,
            device_id=to, device_id_type=MESH,
        )

    def arrived(ref, recv):
        copy(ref, ref, own_send, recv, sib).wait_recv()

    def piece(r, t):
        return cols.at[t, pl.ds(pl.multiple_of(r * rows, rows), rows), :]

    sent, flying = [], {}

    def send(*args):
        c = copy(*args)
        c.start()
        sent.append(c)

    def start_y(t):
        for j in range(1, n_y):
            c = copy(piece(row, t), piece(row, t), y_send.at[j - 1, t], y_recv.at[j - 1, t],
                     y_peers[j - 1])
            c.start()
            flying[t, j] = c

    for t in range(min(AHEAD, tiles)):
        start_y(t)
    if cores > 1:
        ref = cols.at[:, pl.ds(base, rows), :]
        send(ref, ref, own_send, own_recv, sib)

    loads[1 + tiles].wait()
    first = depth - half
    for b in range(pair // BLK):
        keep = mask[pl.ds(first * (strip // BLK) + b, 1), :]
        keep = jnp.broadcast_to(keep, (16, width)).astype(jnp.bfloat16)
        for q in range(b * BLK, (b + 1) * BLK, 16):
            left[q:q + 16, pl.ds(pl.multiple_of(col * width, width), width)] = (
                raw_left[q:q + 16, :] * keep)

    step = width // STEPS

    def slab(c, h, k):
        return left.at[pl.ds(pl.multiple_of(h * strip, strip), strip),
                       pl.ds(pl.multiple_of(c * width + k * step, step), step)]

    for k in range(STEPS):
        for j in range(1, n_col):
            send(slab(col, half, k), slab(col, half, k), x_send.at[j - 1, k],
                 x_recv.at[j - 1, k], x_peers[j - 1])

    def take_x(j, k):
        c = lax.rem(col + n_col - j, n_col)
        arrived(slab(c, half, k), x_recv.at[j - 1, k])
        if share > 1:
            send(slab(c, half, k), slab(c, half, k), z_send.at[j - 1, k],
                 z_recv.at[j - 1, k], mate_at)

    def take_z(j, k):
        if share > 1:
            c = lax.rem(col + n_col - j, n_col)
            arrived(slab(c, 1 - half, k), z_recv.at[j - 1, k])

    def take_y(j, t):
        r = lax.rem(y + n_y - j, n_y) * cores + core
        arrived(piece(r, t), y_recv.at[j - 1, t])
        if cores > 1:
            send(piece(r, t), piece(r, t), s_send.at[j - 1, t], s_recv.at[j - 1, t], sib)

    def make(t):
        if cores > 1:
            for j in range(1, n_y):
                r = lax.rem(y + n_y - j, n_y) * cores + (cores - 1 - core)
                arrived(piece(r, t), s_recv.at[j - 1, t])
        tile = half * tiles + t
        blocks_here = strip // BLK
        for s in range(share):
            who = (1 - half) if s == 0 and share > 1 else half
            begin = pl.multiple_of(who * strip, strip)
            product = jnp.dot(left[pl.ds(begin, strip), :], cols[t],
                              preferred_element_type=jnp.float32)
            for b in range(blocks_here):
                keep = mask_tiles[tile, pl.ds((first + who) * blocks_here + b, 1), :]
                value = (product[b * BLK:(b + 1) * BLK, :] * keep).astype(out.dtype)
                if s == 0 and share > 1:
                    given[t, b * BLK:(b + 1) * BLK, :] = value
                else:
                    made[tile, b * BLK:(b + 1) * BLK, :] = value
            if s == 0 and share > 1:
                send(given.at[t], made.at[tile], o_send.at[t], o_recv.at[t], mate_at)

    for t in range(tiles):
        for j in range(1, n_y):
            take_y(j, t)
            flying[t, j].wait_send()
        if t + AHEAD < tiles:
            start_y(t + AHEAD)
        if t < STEPS:
            for j in range(1, n_col):
                take_x(j, t)
        if t == tiles - 2:
            for k in range(STEPS):
                for j in range(1, n_col):
                    take_z(j, k)
            if cores > 1:
                arrived(cols.at[:, pl.ds(pl.multiple_of(sibling * rows, rows), rows), :], own_recv)
            for q in range(tiles - 1):
                make(q)
    make(tiles - 1)
    if share > 1:
        for t in range(tiles):
            arrived(made.at[(1 - half) * tiles + t], o_recv.at[t])
    for t in range(share * tiles):
        out[:, t * LANES:(t + 1) * LANES] = made[t]
    for c in sent:
        c.wait_send()


def shards(n_row, n_col, n_depth, density, pattern):
    rows, width = density.shape
    strip = rows // n_depth
    cores, share, n_y = layout(n_row, n_depth)
    tiles = width // share // LANES
    dma = pltpu.SemaphoreType.DMA
    i, j = max(n_col - 1, 1), max(n_y - 1, 1)
    bf16 = jnp.bfloat16
    return pl.pallas_call(
        functools.partial(kernel, n_row, n_col, n_depth),
        out_shape=jax.ShapeDtypeStruct((strip, width), bf16),
        in_specs=[pl.BlockSpec(memory_space=pltpu.HBM)] * 2,
        out_specs=pl.BlockSpec(memory_space=pltpu.VMEM),
        scratch_shapes=[
            pltpu.VMEM((tiles, rows, LANES), bf16),
            pltpu.VMEM((share * strip, width), bf16),
            pltpu.VMEM(pattern.shape, jnp.int32),
            pltpu.VMEM((tiles, n_row * rows, LANES), bf16),
            pltpu.VMEM((share * strip, n_col * width), bf16),
            pltpu.VMEM((pattern.shape[0], width), jnp.float32),
            pltpu.VMEM((share * tiles, pattern.shape[0], LANES), jnp.float32),
            pltpu.VMEM((tiles, strip, LANES), bf16),
            pltpu.VMEM((share * tiles, strip, LANES), bf16),
            dma((tiles + 2,)),
            dma((i, STEPS)), dma((i, STEPS)),
            dma((j, tiles)), dma((j, tiles)),
            dma((i, STEPS)), dma((i, STEPS)),
            dma(()), dma(()),
            dma((j, tiles)), dma((j, tiles)),
            dma((tiles,)), dma((tiles,)),
        ],
        compiler_params=pltpu.CompilerParams(
            collective_id=0, has_side_effects=True, vmem_limit_bytes=60 * 1024 * 1024
        ),
    )(density, pattern)


def solution(mesh):
    sizes = [mesh.shape[name] for name in ("row", "col", "depth")]
    return jax.shard_map(
        functools.partial(shards, *sizes),
        mesh=mesh,
        in_specs=(P("row", "col"), P("row", "col")),
        out_specs=P(("row", "depth"), "col"),
        check_vma=False,
    )
```

time: 87.9 us -> 24 us (0.27)
  waiting for transfers between devices: 53.4 us -> 0 us
  Pallas kernels: 0 us -> 22.1 us
  between operations: 13.5 us -> 0.01 us
  blocking collectives: 13.3 us -> 0 us
  matrix products: 2.6 us -> 0 us
  local copies, waits for them, and re-layouts: 4.01 us -> 1.67 us
    all_gather x2 -> x0, waiting for transfers between devices: 52.9 us -> none  [the longest x1 34.7 us: shards(): slab = lax.all_gather(masked, 'col', axis=1, tiled=True)]
    pallas_call x0 -> x1, Pallas kernels: none -> 22.1 us  [shards(): pl.pallas_call(functools.partial(kernel, n_row, n_col, n_depth), out_shap...]
    all_to_all x1 -> x0, blocking collectives: 13.3 us -> none  [shards(): lax.all_to_all(filtered.astype(jnp.bfloat16), 'depth', split_axis=0, conc...]
    dot_general x1 -> x0, matrix products: 2.6 us -> none  [shards(): jnp.dot(slab, lax.all_gather(column_part, 'row', axis=0, tiled=True), pre...]
  transfers between devices with their start and end apart: 2 -> 0, of which waited for: 2 -> 0; matrix products, arithmetic and copies ran while one was open for 1% -> 0% of each run, Pallas kernels for 0% -> 0%
where the time goes in v3:
time: 24 us; the launch traced here: 23.8 us
  Pallas kernels  22.1 us (92%)
  local copies, waits for them, and re-layouts  1.67 us (7%)
    pallas_call x1, Pallas kernels, shards(): pl.pallas_call(functools.partial(kernel, n_row, n_col, n_depth), out_shap...  22.1 us
    unnamed x1, local copies, waits for them, and re-layouts  1.67 us

profile of v3, /device:TPU:0, one launch (start us, length us, event | category | flops | bytes accessed | tf_op | source)
XLA Modules:
  0.0 23.8 jit_solution(5898919193833227312)
XLA Ops:
  0.0 22.1 %shard_map.28 = bf16[128,1024]{1,0:T(8,128)(2,1)} custom-call(bf16[512,1024]{1,0:T(8,128)(2,1)} %density.1, s32[8,16]{1,0:T(8,128)} %pattern.1), custom_call_target="tpu_custom_call" | custom-call | tf_op jit(solution)/shard_map/pallas_call | solution.py:210
  22.1 1.7 %copy.4 = bf16[128,1024]{1,0:T(8,128)(2,1)} copy(bf16[128,1024]{1,0:T(8,128)(2,1)} %shard_map.28) | data formatting | bytes 524288

commit v4 on v3

--- a/solution.py
+++ b/solution.py
@@ -9,7 +9,8 @@
 
 BLK = 64
 LANES = 128
-STEPS = 2
+STEPS = 4
+EARLY = 2
 AHEAD = 2
 MESH = pl.DeviceIdType.MESH
 
@@ -172,23 +173,35 @@
             if s == 0 and share > 1:
                 send(given.at[t], made.at[tile], o_send.at[t], o_recv.at[t], mate_at)
 
+    def forward_x(lo, hi):
+        for k in range(lo, min(hi, STEPS)):
+            for j in range(1, n_col):
+                take_x(j, k)
+
+    def settle():
+        for k in range(STEPS):
+            for j in range(1, n_col):
+                take_z(j, k)
+        if cores > 1:
+            arrived(cols.at[:, pl.ds(pl.multiple_of(sibling * rows, rows), rows), :], own_recv)
+
+    per = STEPS // 2
     for t in range(tiles):
+        if t < 2:
+            forward_x(t * per, t * per + per // 2)
+        if t == tiles - 1:
+            settle()
+            for q in range(EARLY):
+                make(q)
         for j in range(1, n_y):
             take_y(j, t)
             flying[t, j].wait_send()
         if t + AHEAD < tiles:
             start_y(t + AHEAD)
-        if t < STEPS:
-            for j in range(1, n_col):
-                take_x(j, t)
-        if t == tiles - 2:
-            for k in range(STEPS):
-                for j in range(1, n_col):
-                    take_z(j, k)
-            if cores > 1:
-                arrived(cols.at[:, pl.ds(pl.multiple_of(sibling * rows, rows), rows), :], own_recv)
-            for q in range(tiles - 1):
-                make(q)
+        if t < 2:
+            forward_x(t * per + per // 2, t * per + per)
+    for q in range(EARLY, tiles - 1):
+        make(q)
     make(tiles - 1)
     if share > 1:
         for t in range(tiles):
@@ -207,6 +220,8 @@
     dma = pltpu.SemaphoreType.DMA
     i, j = max(n_col - 1, 1), max(n_y - 1, 1)
     bf16 = jnp.bfloat16
+    density = pltpu.with_memory_space_constraint(density, pltpu.HBM)
+    pattern = pltpu.with_memory_space_constraint(pattern, pltpu.HBM)
     return pl.pallas_call(
         functools.partial(kernel, n_row, n_col, n_depth),
         out_shape=jax.ShapeDtypeStruct((strip, width), bf16),
@@ -231,7 +246,7 @@
             dma((tiles,)), dma((tiles,)),
         ],
         compiler_params=pltpu.CompilerParams(
-            collective_id=0, has_side_effects=True, vmem_limit_bytes=60 * 1024 * 1024
+            collective_id=0, has_side_effects=True, vmem_limit_bytes=32 * 1024 * 1024
         ),
     )(density, pattern)
 

time: 24 us -> 22.1 us (0.921)
  local copies, waits for them, and re-layouts: 1.67 us -> 0.71 us
  Pallas kernels: 22.1 us -> 21.3 us
    unnamed x1, local copies, waits for them, and re-layouts: 1.67 us -> 0.71 us
    pallas_call x1, Pallas kernels: 22.1 us -> 21.3 us  [shards(): pl.pallas_call(functools.partial(kernel, n_row, n_col, n_depth), out_shap...]
where the time goes in v4:
time: 22.1 us; the launch traced here: 22 us
  Pallas kernels  21.3 us (96%)
  local copies, waits for them, and re-layouts  0.71 us (3%)
    pallas_call x1, Pallas kernels, shards(): pl.pallas_call(functools.partial(kernel, n_row, n_col, n_depth), out_shap...  21.3 us
    unnamed x1, local copies, waits for them, and re-layouts  0.71 us

profile of v4, /device:TPU:0, one launch (start us, length us, event | category | flops | bytes accessed | tf_op | source)
XLA Modules:
  0.0 22.0 jit_solution(8100303137116886337)
XLA Ops:
  0.0 21.3 %shard_map.28 = bf16[128,1024]{1,0:T(8,128)(2,1)S(1)} custom-call(bf16[512,1024]{1,0:T(8,128)(2,1)} %density.1, s32[8,16]{1,0:T(8,128)} %pattern.1), custom_call_target="tpu_custom_call" | custom-call | tf_op jit(solution)/shard_map/pallas_call | solution.py:225
  21.3 0.7 %copy.4 = bf16[128,1024]{1,0:T(8,128)(2,1)} copy(bf16[128,1024]{1,0:T(8,128)(2,1)S(1)} %shard_map.28) | data formatting | bytes 524288

commit v5 on v4

--- a/solution.py
+++ b/solution.py
@@ -151,14 +151,14 @@
         if cores > 1:
             send(piece(r, t), piece(r, t), s_send.at[j - 1, t], s_recv.at[j - 1, t], sib)
 
-    def make(t):
-        if cores > 1:
+    def make(t, which):
+        if cores > 1 and which[0] == 0:
             for j in range(1, n_y):
                 r = lax.rem(y + n_y - j, n_y) * cores + (cores - 1 - core)
                 arrived(piece(r, t), s_recv.at[j - 1, t])
         tile = half * tiles + t
         blocks_here = strip // BLK
-        for s in range(share):
+        for s in which:
             who = (1 - half) if s == 0 and share > 1 else half
             begin = pl.multiple_of(who * strip, strip)
             product = jnp.dot(left[pl.ds(begin, strip), :], cols[t],
@@ -192,7 +192,7 @@
         if t == tiles - 1:
             settle()
             for q in range(EARLY):
-                make(q)
+                make(q, range(share))
         for j in range(1, n_y):
             take_y(j, t)
             flying[t, j].wait_send()
@@ -201,8 +201,11 @@
         if t < 2:
             forward_x(t * per + per // 2, t * per + per)
     for q in range(EARLY, tiles - 1):
-        make(q)
-    make(tiles - 1)
+        make(q, (0,))
+    make(tiles - 1, (0,))
+    if share > 1:
+        for q in range(EARLY, tiles):
+            make(q, (1,))
     if share > 1:
         for t in range(tiles):
             arrived(made.at[(1 - half) * tiles + t], o_recv.at[t])

time: 22.1 us -> 21.7 us (0.982)
  Pallas kernels: 21.3 us -> 20.8 us
    pallas_call x1, Pallas kernels: 21.3 us -> 20.8 us  [shards(): pl.pallas_call(functools.partial(kernel, n_row, n_col, n_depth), out_shap...]
where the time goes in v5:
time: 21.7 us; the launch traced here: 21.6 us
  Pallas kernels  20.8 us (96%)
  local copies, waits for them, and re-layouts  0.71 us (3%)
    pallas_call x1, Pallas kernels, shards(): pl.pallas_call(functools.partial(kernel, n_row, n_col, n_depth), out_shap...  20.8 us
    unnamed x1, local copies, waits for them, and re-layouts  0.71 us

profile of v5, /device:TPU:0, one launch (start us, length us, event | category | flops | bytes accessed | tf_op | source)
XLA Modules:
  0.0 21.6 jit_solution(8665261532713384834)
XLA Ops:
  0.0 20.8 %shard_map.28 = bf16[128,1024]{1,0:T(8,128)(2,1)S(1)} custom-call(bf16[512,1024]{1,0:T(8,128)(2,1)} %density.1, s32[8,16]{1,0:T(8,128)} %pattern.1), custom_call_target="tpu_custom_call" | custom-call | tf_op jit(solution)/shard_map/pallas_call | solution.py:228
  20.8 0.7 %copy.4 = bf16[128,1024]{1,0:T(8,128)(2,1)} copy(bf16[128,1024]{1,0:T(8,128)(2,1)S(1)} %shard_map.28) | data formatting | bytes 524288

commit v6 on v5

--- a/solution.py
+++ b/solution.py
@@ -10,7 +10,7 @@
 BLK = 64
 LANES = 128
 STEPS = 4
-EARLY = 2
+EARLY = 3
 AHEAD = 2
 MESH = pl.DeviceIdType.MESH
 
@@ -192,7 +192,7 @@
         if t == tiles - 1:
             settle()
             for q in range(EARLY):
-                make(q, range(share))
+                make(q, (0,))
         for j in range(1, n_y):
             take_y(j, t)
             flying[t, j].wait_send()
@@ -204,7 +204,7 @@
         make(q, (0,))
     make(tiles - 1, (0,))
     if share > 1:
-        for q in range(EARLY, tiles):
+        for q in range(tiles):
             make(q, (1,))
     if share > 1:
         for t in range(tiles):

time: 21.7 us -> 22.3 us (1.028)
  Pallas kernels: 20.8 us -> 21.4 us
    pallas_call x1, Pallas kernels: 20.8 us -> 21.4 us  [shards(): pl.pallas_call(functools.partial(kernel, n_row, n_col, n_depth), out_shap...]
where the time goes in v6:
time: 22.3 us; the launch traced here: 22.1 us
  Pallas kernels  21.4 us (96%)
  local copies, waits for them, and re-layouts  0.71 us (3%)
    pallas_call x1, Pallas kernels, shards(): pl.pallas_call(functools.partial(kernel, n_row, n_col, n_depth), out_shap...  21.4 us
    unnamed x1, local copies, waits for them, and re-layouts  0.71 us

profile of v6, /device:TPU:0, one launch (start us, length us, event | category | flops | bytes accessed | tf_op | source)
XLA Modules:
  0.0 22.1 jit_solution(17842153751232428671)
XLA Ops:
  0.0 21.4 %shard_map.28 = bf16[128,1024]{1,0:T(8,128)(2,1)S(1)} custom-call(bf16[512,1024]{1,0:T(8,128)(2,1)} %density.1, s32[8,16]{1,0:T(8,128)} %pattern.1), custom_call_target="tpu_custom_call" | custom-call | tf_op jit(solution)/shard_map/pallas_call | solution.py:228
  21.4 0.7 %copy.4 = bf16[128,1024]{1,0:T(8,128)(2,1)} copy(bf16[128,1024]{1,0:T(8,128)(2,1)S(1)} %shard_map.28) | data formatting | bytes 524288
